TPU v7x, 32 devices: a whole 2x2x4 slice. The times are simulated.
32 devices in a mesh: dp: 8 (over y, x, core), fsdp: 4 (over z).
Axes of the slice: x: 2, y: 2, z: 4, core: 2. Of those that a mesh axis runs over, the one named last changes fastest.
Arguments:
- hidden_in: bfloat16 [2, 12288, 768], P(None, ('dp', 'fsdp')), may hold values from -6 to 6
- grad_out: bfloat16 [2, 12288, 768], P(None, ('dp', 'fsdp')), may hold values from -6 to 6
- gain_attn: bfloat16 [768], P(('dp', 'fsdp')), may hold values from 0.099609375 to 1.8984375
- gain_ffn: bfloat16 [768], P(('dp', 'fsdp')), may hold values from 0.099609375 to 1.8984375
- rel_bias: bfloat16 [384], P(('dp', 'fsdp')), may hold values from -4 to 4
- w_query: bfloat16 [768, 768], P(('dp', 'fsdp')), may hold values from -0.046875 to 0.046875
- w_key: bfloat16 [768, 768], P(('dp', 'fsdp')), may hold values from -0.21875 to 0.21875
- w_value: bfloat16 [768, 768], P(('dp', 'fsdp')), may hold values from -0.21875 to 0.21875
- w_output: bfloat16 [768, 768], P(('dp', 'fsdp')), may hold values from -0.875 to 0.875
- w_inner: bfloat16 [768, 3072], P(('dp', 'fsdp')), may hold values from -0.21875 to 0.21875
- w_outer: bfloat16 [3072, 768], P(('dp', 'fsdp')), may hold values from -0.15625 to 0.15625
- dealing: int32 [2, 8, 1536], P(None, 'dp'), may hold values from 0 to 1535, as said below
- lengths: int32 [2, 8, 4], P(None, 'dp'), may hold values from 1 to 768, 1536 in all within a row
- bucket_table: int32 [257], replicated, may hold values from 0 to 31, as said below
Outputs:
- hidden_out: float32 [2, 12288, 768], P(None, ('dp', 'fsdp'))
- grad_in: float32 [2, 12288, 768], P(None, ('dp', 'fsdp'))
- grad_gain_attn: float32 [768], P(('dp', 'fsdp'))
- grad_gain_ffn: float32 [768], P(('dp', 'fsdp'))
- grad_rel_bias: float32 [384], P(('dp', 'fsdp'))
- grad_query: float32 [768, 768], P(('dp', 'fsdp'))
- grad_key: float32 [768, 768], P(('dp', 'fsdp'))
- grad_value: float32 [768, 768], P(('dp', 'fsdp'))
- grad_output: float32 [768, 768], P(('dp', 'fsdp'))
- grad_inner: float32 [768, 3072], P(('dp', 'fsdp'))
- grad_outer: float32 [3072, 768], P(('dp', 'fsdp'))
Inputs may be any that keep to these rules, and one draw needn't show every extreme that they name: Each row dealing[m, g] is a permutation of 0 .. 1535. For t < 96, the entry at dealt place 384 * e + 96 * s + t lies in 384 * s .. 384 * s + 383. Each row lengths[m, g] sums to 1536; its longest entry is 768. `bucket_table`: entry 128 + r is the bucket of distance r. For r <= 0 it lies in 0 .. 15, for r > 0 in 17 .. 31, never falling as |r| grows on either side; distances |r| < 8 have buckets of their own, and every bucket but 32 / 2 is used.
All inputs are finite; a program needn't handle non-finite values.
Results may differ from a plain program's by a relative error of at most 0.019.
Values may be sent and summed in bfloat16 or wider, within the bound.
A program may use at most 256 MiB of HBM per device.

v0:
```python
import math

import jax
import jax.numpy as jnp
from jax import lax
from jax.sharding import PartitionSpec as P

H = 12
BUCKETS = 32


EPSILON = 1e-06
NEG_FILL = -1e30


def token_places(deal_order, lengths):
    seq_ends = jnp.cumsum(lengths)
    starts = seq_ends - lengths
    inside = (deal_order[:, None] >= starts[None, :]).astype(jnp.int32)
    segment = jnp.sum(inside, axis=1) - 1
    picked = (segment[:, None] == jnp.arange(lengths.shape[0], dtype=jnp.int32)[None, :]).astype(
        jnp.int32
    )
    position = deal_order - jnp.sum(picked * starts[None, :], axis=1)
    return (segment, position)


def rms_scale(rows_in):
    return lax.rsqrt(jnp.mean(rows_in * rows_in, axis=1, keepdims=True) + EPSILON)


def gelu_slope(values):
    normal_cdf = 0.5 * (1.0 + jax.scipy.special.erf(values * (1.0 / math.sqrt(2.0))))
    normal_pdf = jnp.exp(-0.5 * values * values) * (1.0 / math.sqrt(2.0 * math.pi))
    return normal_cdf + values * normal_pdf


def norm_back(rows_in, scale, gain, grad_normed):
    scaled_grad = grad_normed * gain
    grad_gain = jnp.sum(grad_normed * rows_in * scale, axis=0)
    grad_rows = scale * scaled_grad - rows_in * scale * scale * scale * jnp.mean(
        scaled_grad * rows_in, axis=1, keepdims=True
    )
    return (grad_rows, grad_gain)


def key_layout(key_all, value_all, segment, position, head_count):
    rows_all = key_all.shape[0]
    block_rows = 512
    blocks = rows_all // block_rows
    return (
        key_all.reshape(blocks, block_rows, head_count, -1),
        value_all.reshape(blocks, block_rows, head_count, -1),
        segment.reshape(blocks, block_rows),
        position.reshape(blocks, block_rows),
    )


def block_scores(
    queries,
    key_block,
    seg_query,
    pos_query,
    seg_block,
    pos_block,
    rel_bucket,
    bucket_edges,
    max_offset,
):
    lower_edge, upper_edge = bucket_edges
    raw_scores = jnp.einsum("qhd,khd->hqk", queries, key_block, preferred_element_type=jnp.float32)
    offset = jnp.clip(pos_block[None, :] - pos_query[:, None], -max_offset, max_offset)
    bucket_hit = (
        (offset[:, :, None] >= lower_edge[None, None, :])
        & (offset[:, :, None] <= upper_edge[None, None, :])
    ).astype(jnp.float32)
    bias = jnp.einsum(
        "qkb,bh->hqk",
        bucket_hit,
        rel_bucket,
        precision=lax.Precision.HIGHEST,
        preferred_element_type=jnp.float32,
    )
    same_seq = (seg_query[:, None] == seg_block[None, :])[None]
    return (raw_scores + bias, same_seq, bucket_hit)


def attend(queries, layout, seg_query, pos_query, rel_bucket, bucket_edges, max_offset):
    key_blocks, value_blocks, seg_blocks, pos_blocks = layout
    query_count, head_count, head_size = queries.shape

    def measure(carry, block):
        row_top, row_total = carry
        key_block, seg_block, pos_block = block
        scores, same_seq, _ = block_scores(
            queries,
            key_block,
            seg_query,
            pos_query,
            seg_block,
            pos_block,
            rel_bucket,
            bucket_edges,
            max_offset,
        )
        scores = jnp.where(same_seq, scores, NEG_FILL)
        new_top = jnp.maximum(row_top, jnp.max(scores, axis=2))
        weights_now = jnp.where(same_seq, jnp.exp(scores - new_top[:, :, None]), 0.0)
        row_total = row_total * jnp.exp(row_top - new_top) + jnp.sum(weights_now, axis=2)
        return ((new_top, row_total), None)

    start = (
        jnp.full((head_count, query_count), NEG_FILL, jnp.float32),
        jnp.zeros((head_count, query_count), jnp.float32),
    )
    (row_top, row_total), _ = lax.scan(measure, start, (key_blocks, seg_blocks, pos_blocks))
    log_total = row_top + jnp.log(row_total)

    def collect(summed, block):
        key_block, value_block, seg_block, pos_block = block
        scores, same_seq, _ = block_scores(
            queries,
            key_block,
            seg_query,
            pos_query,
            seg_block,
            pos_block,
            rel_bucket,
            bucket_edges,
            max_offset,
        )
        probs = jnp.where(same_seq, jnp.exp(scores - log_total[:, :, None]), 0.0).astype(
            jnp.bfloat16
        )
        return (
            summed
            + jnp.einsum("hqk,khd->qhd", probs, value_block, preferred_element_type=jnp.float32),
            None,
        )

    attended_f, _ = lax.scan(
        collect, jnp.zeros((query_count, head_count, head_size), jnp.float32), layout
    )
    return (attended_f, log_total)


def attend_back(
    queries,
    layout,
    seg_query,
    pos_query,
    rel_bucket,
    bucket_edges,
    max_offset,
    log_total,
    d_attended,
    row_delta,
):

    def step(carry, block):
        d_queries, d_buckets = carry
        key_block, value_block, seg_block, pos_block = block
        scores, same_seq, bucket_hit = block_scores(
            queries,
            key_block,
            seg_query,
            pos_query,
            seg_block,
            pos_block,
            rel_bucket,
            bucket_edges,
            max_offset,
        )
        probs_f = jnp.where(same_seq, jnp.exp(scores - log_total[:, :, None]), 0.0)
        d_probs = jnp.einsum(
            "qhd,khd->hqk", d_attended, value_block, preferred_element_type=jnp.float32
        )
        d_scores = (probs_f * (d_probs - row_delta[:, :, None])).astype(jnp.bfloat16)
        d_queries = d_queries + jnp.einsum(
            "hqk,khd->qhd", d_scores, key_block, preferred_element_type=jnp.float32
        )
        d_buckets = d_buckets + jnp.einsum(
            "hqk,qkb->bh",
            d_scores,
            bucket_hit.astype(jnp.bfloat16),
            preferred_element_type=jnp.float32,
        )
        d_values = jnp.einsum(
            "hqk,qhd->khd",
            probs_f.astype(jnp.bfloat16),
            d_attended,
            preferred_element_type=jnp.float32,
        )
        d_keys = jnp.einsum("hqk,qhd->khd", d_scores, queries, preferred_element_type=jnp.float32)
        return ((d_queries, d_buckets), (d_keys, d_values))

    start = (jnp.zeros(queries.shape, jnp.float32), jnp.zeros(rel_bucket.shape, jnp.float32))
    (d_queries, d_buckets), key_terms = lax.scan(step, start, layout)
    return (d_queries, key_terms, d_buckets)


def on_device(
    hidden_in,
    grad_out,
    gain_attn,
    gain_ffn,
    rel_bias,
    w_query,
    w_key,
    w_value,
    w_output,
    w_inner,
    w_outer,
    dealing,
    lengths,
    bucket_table,
):
    micro_count, tok_rows, model_width = hidden_in.shape
    group_size = lax.axis_size("fsdp")
    slot_rows = tok_rows // group_size
    own_index = lax.axis_index("fsdp")
    max_offset = (bucket_table.shape[0] - 1) // 2
    bucket_count = BUCKETS
    head_count = H
    offsets_all = jnp.arange(bucket_table.shape[0], dtype=jnp.int32) - max_offset
    matches = bucket_table[:, None] == jnp.arange(bucket_count, dtype=jnp.int32)[None, :]
    lower_edge = jnp.min(jnp.where(matches, offsets_all[:, None], 2 * max_offset + 2), axis=0)
    upper_edge = jnp.max(jnp.where(matches, offsets_all[:, None], -2 * max_offset - 2), axis=0)
    bucket_edges = (lower_edge, upper_edge)
    hidden_units = w_inner.shape[1]
    acc_gain_one = jnp.zeros((model_width,), jnp.float32)
    acc_gain_two = jnp.zeros((model_width,), jnp.float32)
    acc_buckets = jnp.zeros((bucket_count, head_count), jnp.float32)
    acc_query = jnp.zeros((model_width, model_width), jnp.float32)
    acc_key = jnp.zeros((model_width, model_width), jnp.float32)
    acc_value = jnp.zeros((model_width, model_width), jnp.float32)
    acc_output = jnp.zeros((model_width, model_width), jnp.float32)
    acc_inner = jnp.zeros((model_width, hidden_units), jnp.float32)
    acc_outer = jnp.zeros((hidden_units, model_width), jnp.float32)
    outputs_list = []
    grads_list = []
    for micro_idx in range(micro_count):
        weights_now = (
            lax.all_gather(gain_attn, ("dp", "fsdp"), axis=0, tiled=True),
            lax.all_gather(gain_ffn, ("dp", "fsdp"), axis=0, tiled=True),
            lax.all_gather(rel_bias, ("dp", "fsdp"), axis=0, tiled=True),
            lax.all_gather(w_query, ("dp", "fsdp"), axis=0, tiled=True),
            lax.all_gather(w_key, ("dp", "fsdp"), axis=0, tiled=True),
            lax.all_gather(w_value, ("dp", "fsdp"), axis=0, tiled=True),
            lax.all_gather(w_output, ("dp", "fsdp"), axis=0, tiled=True),
            lax.all_gather(w_inner, ("dp", "fsdp"), axis=0, tiled=True),
            lax.all_gather(w_outer, ("dp", "fsdp"), axis=0, tiled=True),
        )
        gain_one = weights_now[0].astype(jnp.float32)
        gain_two = weights_now[1].astype(jnp.float32)
        rel_bucket = weights_now[2].astype(jnp.float32).reshape(bucket_count, head_count)
        query_weight, key_weight, value_weight, output_weight, inner_weight, outer_weight = (
            weights_now[3:]
        )
        deal_order = dealing[micro_idx, 0]
        segment, position = token_places(deal_order, lengths[micro_idx, 0])
        seg_query = lax.dynamic_slice_in_dim(segment, own_index * tok_rows, tok_rows)
        pos_query = lax.dynamic_slice_in_dim(position, own_index * tok_rows, tok_rows)
        take_rows = (
            lax.dynamic_slice_in_dim(
                deal_order.reshape(group_size, tok_rows), own_index * slot_rows, slot_rows, 1
            )
            - own_index * tok_rows
        ).reshape(tok_rows)
        dealt = lax.all_to_all(
            jnp.take(hidden_in[micro_idx], take_rows, axis=0),
            "fsdp",
            split_axis=0,
            concat_axis=0,
            tiled=True,
        )
        dealt_rows = dealt.astype(jnp.float32)
        scale_one = rms_scale(dealt_rows)
        normed1 = (dealt_rows * scale_one * gain_one).astype(jnp.bfloat16)
        queries = jnp.dot(normed1, query_weight, preferred_element_type=jnp.float32).astype(
            jnp.bfloat16
        )
        key_rows = jnp.dot(normed1, key_weight, preferred_element_type=jnp.float32).astype(
            jnp.bfloat16
        )
        value_rows = jnp.dot(normed1, value_weight, preferred_element_type=jnp.float32).astype(
            jnp.bfloat16
        )
        key_all, value_all = (
            lax.all_gather(key_rows, "fsdp", axis=0, tiled=True),
            lax.all_gather(value_rows, "fsdp", axis=0, tiled=True),
        )
        layout = key_layout(key_all, value_all, segment, position, head_count)
        queries_heads = queries.reshape(tok_rows, head_count, -1)
        attended_f, log_total = attend(
            queries_heads, layout, seg_query, pos_query, rel_bucket, bucket_edges, max_offset
        )
        attended = attended_f.reshape(tok_rows, model_width).astype(jnp.bfloat16)
        mid = dealt_rows + jnp.dot(attended, output_weight, preferred_element_type=jnp.float32)
        scale_two = rms_scale(mid)
        normed2 = (mid * scale_two * gain_two).astype(jnp.bfloat16)
        inner_act = jnp.dot(normed2, inner_weight, preferred_element_type=jnp.float32)
        active = jax.nn.gelu(inner_act, approximate=False).astype(jnp.bfloat16)
        result = mid + jnp.dot(active, outer_weight, preferred_element_type=jnp.float32)
        outputs_list.append(result)
        weights_back = (
            lax.all_gather(gain_attn, ("dp", "fsdp"), axis=0, tiled=True),
            lax.all_gather(gain_ffn, ("dp", "fsdp"), axis=0, tiled=True),
            lax.all_gather(rel_bias, ("dp", "fsdp"), axis=0, tiled=True),
            lax.all_gather(w_query, ("dp", "fsdp"), axis=0, tiled=True),
            lax.all_gather(w_key, ("dp", "fsdp"), axis=0, tiled=True),
            lax.all_gather(w_value, ("dp", "fsdp"), axis=0, tiled=True),
            lax.all_gather(w_output, ("dp", "fsdp"), axis=0, tiled=True),
            lax.all_gather(w_inner, ("dp", "fsdp"), axis=0, tiled=True),
            lax.all_gather(w_outer, ("dp", "fsdp"), axis=0, tiled=True),
        )
        query_weight, key_weight, value_weight, output_weight, inner_weight, outer_weight = (
            weights_back[3:]
        )
        grad_top = grad_out[micro_idx]
        acc_outer = acc_outer + jnp.einsum(
            "tf,td->fd", active, grad_top, preferred_element_type=jnp.float32
        )
        d_active = jnp.einsum(
            "td,fd->tf", grad_top, outer_weight, preferred_element_type=jnp.float32
        )
        d_inner = (d_active * gelu_slope(inner_act)).astype(jnp.bfloat16)
        acc_inner = acc_inner + jnp.einsum(
            "td,tf->df", normed2, d_inner, preferred_element_type=jnp.float32
        )
        d_normed2 = jnp.einsum(
            "tf,df->td", d_inner, inner_weight, preferred_element_type=jnp.float32
        )
        d_mid_norm, d_gain_two = norm_back(mid, scale_two, gain_two, d_normed2)
        acc_gain_two = acc_gain_two + d_gain_two
        d_mid = grad_top.astype(jnp.float32) + d_mid_norm
        d_branch = d_mid.astype(jnp.bfloat16)
        acc_output = acc_output + jnp.einsum(
            "td,te->de", attended, d_branch, preferred_element_type=jnp.float32
        )
        d_attended = jnp.einsum(
            "te,de->td", d_branch, output_weight, preferred_element_type=jnp.float32
        ).astype(jnp.bfloat16)
        d_attended_heads = d_attended.reshape(tok_rows, head_count, -1)
        row_delta = jnp.sum(d_attended_heads.astype(jnp.float32) * attended_f, axis=2).T
        key_back, value_back = (
            lax.all_gather(key_rows, "fsdp", axis=0, tiled=True),
            lax.all_gather(value_rows, "fsdp", axis=0, tiled=True),
        )
        layout_back = key_layout(key_back, value_back, segment, position, head_count)
        d_queries, key_terms, d_buckets = attend_back(
            queries_heads,
            layout_back,
            seg_query,
            pos_query,
            rel_bucket,
            bucket_edges,
            max_offset,
            log_total,
            d_attended_heads,
            row_delta,
        )
        d_keys, d_values = key_terms
        group_rows = d_keys.shape[0] * d_keys.shape[1]
        d_keys_own, d_values_own = (
            lax.psum_scatter(
                d_keys.reshape(group_rows, model_width).astype(jnp.bfloat16),
                "fsdp",
                scatter_dimension=0,
                tiled=True,
            ).astype(jnp.float32),
            lax.psum_scatter(
                d_values.reshape(group_rows, model_width).astype(jnp.bfloat16),
                "fsdp",
                scatter_dimension=0,
                tiled=True,
            ).astype(jnp.float32),
        )
        acc_buckets = acc_buckets + d_buckets
        d_queries_low = d_queries.reshape(tok_rows, model_width).astype(jnp.bfloat16)
        d_keys_low = d_keys_own.astype(jnp.bfloat16)
        d_values_low = d_values_own.astype(jnp.bfloat16)
        acc_query = acc_query + jnp.einsum(
            "td,te->de", normed1, d_queries_low, preferred_element_type=jnp.float32
        )
        acc_key = acc_key + jnp.einsum(
            "td,te->de", normed1, d_keys_low, preferred_element_type=jnp.float32
        )
        acc_value = acc_value + jnp.einsum(
            "td,te->de", normed1, d_values_low, preferred_element_type=jnp.float32
        )
        d_normed1 = (
            jnp.einsum("te,de->td", d_queries_low, query_weight, preferred_element_type=jnp.float32)
            + jnp.einsum("te,de->td", d_keys_low, key_weight, preferred_element_type=jnp.float32)
            + jnp.einsum(
                "te,de->td", d_values_low, value_weight, preferred_element_type=jnp.float32
            )
        )
        d_rows_norm, d_gain_one = norm_back(dealt_rows, scale_one, gain_one, d_normed1)
        acc_gain_one = acc_gain_one + d_gain_one
        d_dealt = d_mid + d_rows_norm
        returned = lax.all_to_all(
            d_dealt.astype(jnp.bfloat16), "fsdp", split_axis=0, concat_axis=0, tiled=True
        ).astype(d_dealt.dtype)
        grads_list.append(jnp.zeros_like(returned).at[take_rows].set(returned))
    acc_rel = acc_buckets.reshape(-1)
    summed = (
        lax.psum_scatter(acc_gain_one, ("dp", "fsdp"), scatter_dimension=0, tiled=True),
        lax.psum_scatter(acc_gain_two, ("dp", "fsdp"), scatter_dimension=0, tiled=True),
        lax.psum_scatter(acc_rel, ("dp", "fsdp"), scatter_dimension=0, tiled=True),
        lax.psum_scatter(acc_query, ("dp", "fsdp"), scatter_dimension=0, tiled=True),
        lax.psum_scatter(acc_key, ("dp", "fsdp"), scatter_dimension=0, tiled=True),
        lax.psum_scatter(acc_value, ("dp", "fsdp"), scatter_dimension=0, tiled=True),
        lax.psum_scatter(acc_output, ("dp", "fsdp"), scatter_dimension=0, tiled=True),
        lax.psum_scatter(acc_inner, ("dp", "fsdp"), scatter_dimension=0, tiled=True),
        lax.psum_scatter(acc_outer, ("dp", "fsdp"), scatter_dimension=0, tiled=True),
    )
    return (
        jnp.stack(outputs_list),
        jnp.stack(grads_list),
        summed[0],
        summed[1],
        summed[2],
        summed[3],
        summed[4],
        summed[5],
        summed[6],
        summed[7],
        summed[8],
    )


def solution(mesh):
    placed = (
        P(None, ("dp", "fsdp"), None),
        P(None, ("dp", "fsdp"), None),
        P(("dp", "fsdp")),
        P(("dp", "fsdp")),
        P(("dp", "fsdp")),
        P(("dp", "fsdp"), None),
        P(("dp", "fsdp"), None),
        P(("dp", "fsdp"), None),
        P(("dp", "fsdp"), None),
        P(("dp", "fsdp"), None),
        P(("dp", "fsdp"), None),
        P(None, "dp", None),
        P(None, "dp", None),
        P(),
    )
    return jax.shard_map(
        on_device,
        mesh=mesh,
        in_specs=placed,
        out_specs=(
            P(None, ("dp", "fsdp"), None),
            P(None, ("dp", "fsdp"), None),
            P(("dp", "fsdp")),
            P(("dp", "fsdp")),
            P(("dp", "fsdp")),
            P(("dp", "fsdp"), None),
            P(("dp", "fsdp"), None),
            P(("dp", "fsdp"), None),
            P(("dp", "fsdp"), None),
            P(("dp", "fsdp"), None),
            P(("dp", "fsdp"), None),
        ),
        check_vma=False,
    )
```

profile of v0, /device:TPU:0, one launch (start us, length us, event | category | flops | bytes accessed | tf_op | source)
XLA Modules:
  0.0 2021.3 jit_solution(14055427984738968390)
XLA Ops:
  24.4 12.7 all-to-all-done
  41.4 40.9 %all-reduce.7 = (bf16[768]{0:T(1024)(128)(2,1)S(1)}, bf16[384]{0:T(512)(128)(2,1)}, bf16[768]{0:T(1024)(128)(2,1)}) all-reduce(bf16[768]{0:T(1024)(128)(2,1)S(1)} %dynamic-update-slice, bf16[384]{0:T(512)(128)(2,1)S(1)} %dynamic-update-slice.1, bf16[768]{0:T(1024)(128)(2,1)S(1)} %dynamic-update-slice.2), channel_id=1, replica_groups=mesh['dp'=8,'fsdp'=4] {'dp','fsdp'}, use_global_device_ids=true, to_apply=%add | all-reduce | flops 1920 | bytes 7680
  86.5 44.4 %all-gather.15.cloned.1.call-done = bf16[768,768]{1,0:T(8,128)(2,1)} async-done(((bf16[24,768]{1,0:T(8,128)(2,1)}), bf16[768,768]{1,0:T(8,128)(2,1)}) %all-gather.15.cloned.1.call-update) | async-done | bytes 1179664 | tf_op jit(solution)/shard_map/all_gather | solution.py:248
  145.6 41.2 %all-gather.19.cloned.1.call-done = bf16[768,768]{1,0:T(8,128)(2,1)} async-done(((bf16[24,768]{1,0:T(8,128)(2,1)}), bf16[768,768]{1,0:T(8,128)(2,1)}) %all-gather.19.cloned.1.call-update) | async-done | bytes 1179664 | tf_op jit(solution)/shard_map/all_gather | solution.py:247
  190.9 47.4 %all-gather.27.cloned.1.call-done = bf16[1536,768]{1,0:T(8,128)(2,1)} async-done(((bf16[384,768]{1,0:T(8,128)(2,1)}), bf16[1536,768]{1,0:T(8,128)(2,1)}) %all-gather.27.cloned.1.call-update) | async-done | bytes 2359312 | tf_op jit(solution)/shard_map/all_gather | solution.py:291
  254.0 35.6 %all-gather.29.cloned.1.call-done = bf16[1536,768]{1,0:T(8,128)(2,1)} async-done(((bf16[384,768]{1,0:T(8,128)(2,1)}), bf16[1536,768]{1,0:T(8,128)(2,1)}) %all-gather.29.cloned.1.call-update) | async-done | bytes 2359312 | tf_op jit(solution)/shard_map/all_gather | solution.py:290
  304.4 127.8 %while.84 = (s32[]{:T(128)}, f32[12,384]{1,0:T(8,128)S(1)}, f32[12,384]{1,0:T(8,128)S(1)}, s32[384]{0:T(512)S(1)}, s32[3,512]{1,0:T(4,128)}, /*index=5*/bf16[3,5...) while((s32[]{:T(128)}, f32[12,384]{1,0:T(8,128)S(1)}, ...), condition=%wide.region_20.22_spmd.clone, body=%wide.region_17.21_spmd.clone.sunk | while | flops 1246321152 | bytes 69856152 | solution.py:116
  432.2 99.2 %while.85 = (s32[]{:T(128)}, f32[384,12,64]{0,2,1:T(8,128)}, bf16[3,512,12,64]{1,3,2,0:T(8,128)(2,1)}, s32[384]{0:T(512)S(1)}, s32[3,512]{1,0:T(4,128)}, /*index...) while((s32[]{:T(128)}, f32[384,12,64]{0,2,1:T(8,128)}, ...), condition=%wide.region_22.24_spmd.clone, body=%wide.region_21.23_spmd.clone.sunk | while | flops 1539440640 | bytes 44280224 | solution.py:141
  564.7 128.1 %while.82 = (s32[]{:T(128)}, f32[12,384]{1,0:T(8,128)S(1)}, f32[12,384]{1,0:T(8,128)S(1)}, s32[384]{0:T(512)S(1)}, s32[3,512]{1,0:T(4,128)}, /*index=5*/bf16[3,5...) while((s32[]{:T(128)}, f32[12,384]{1,0:T(8,128)S(1)}, ...), condition=%wide.region_9.11_spmd.clone, body=%wide.region_6.10_spmd.clone.sunk | while | flops 1246321152 | bytes 69856152 | solution.py:116
  566.0 11.9 fusion.396
  692.8 98.5 %while.83 = (s32[]{:T(128)}, f32[384,12,64]{0,2,1:T(8,128)}, bf16[3,512,12,64]{1,3,2,0:T(8,128)(2,1)}, s32[384]{0:T(512)S(1)}, s32[3,512]{1,0:T(4,128)}, /*index...) while((s32[]{:T(128)}, f32[384,12,64]{0,2,1:T(8,128)}, ...), condition=%wide.region_11.13_spmd.clone, body=%wide.region_10.12_spmd.clone.sunk | while | flops 1539440640 | bytes 44280224 | solution.py:141
  801.0 15.4 fusion.167
  824.2 13.3 fusion.164
  863.2 137.3 %while.86 = (s32[]{:T(128)}, f32[384,12,64]{0,2,1:T(8,128)}, f32[32,12]{0,1:T(8,128)}, bf16[3,512,12,64]{1,3,2,0:T(8,128)(2,1)}, bf16[3,512,12,64]{1,3,2,0:T(8,1...) while((s32[]{:T(128)}, f32[384,12,64]{0,2,1:T(8,128)}, ...), condition=%wide.region_27.29_spmd.clone, body=%wide.region_26.28_spmd.clone.sunk | while | flops 2634941184 | bytes 184630320 | solution.py:198
  1020.6 124.0 %while.87 = (s32[]{:T(128)}, f32[384,12,64]{0,2,1:T(8,128)}, f32[32,12]{0,1:T(8,128)}, bf16[3,512,12,64]{1,3,2,0:T(8,128)(2,1)}, bf16[3,512,12,64]{1,3,2,0:T(8,1...) while((s32[]{:T(128)}, f32[384,12,64]{0,2,1:T(8,128)}, ...), condition=%wide.region_35.37_spmd.clone, body=%wide.region_34.36_spmd.clone.sunk | while | flops 2634941184 | bytes 184629776 | solution.py:198
  1214.0 43.9 %reduce-scatter.33.cloned.1.call-done = bf16[384,768]{1,0:T(8,128)(2,1)} async-done(((bf16[1536,768]{1,0:T(8,128)(2,1)}), bf16[384,768]{1,0:T(8,128)(2,1)}) %reduce-scatter.33.cloned.1.call-update) | async-done | bytes 589840
  1261.4 46.3 %reduce-scatter.37.cloned.1.call-done = bf16[384,768]{1,0:T(8,128)(2,1)} async-done(((bf16[1536,768]{1,0:T(8,128)(2,1)}), bf16[384,768]{1,0:T(8,128)(2,1)}) %reduce-scatter.37.cloned.1.call-update) | async-done | bytes 589840
  1347.6 15.2 all-to-all-done.3
  1380.9 41.0 %all-reduce.6 = (f32[768]{0:T(1024)S(1)}, f32[768]{0:T(1024)S(1)}, f32[384]{0:T(512)S(1)}) all-reduce(f32[768]{0:T(1024)S(1)} %add.284, f32[768]{0:T(1024)S(1)} %add.285, f32[384]{0:T(512)S(1)} %reshape.740), channel_id=6, replica_groups=mesh['dp'=8,'fsdp'=4] {'dp','fsdp'}, use_global_device_ids=true, to_apply=%region_42.44.clone | all-reduce | flops 1920 | bytes 15360
  1430.3 92.7 %reduce-scatter.25.cloned.1.call-done = f32[24,768]{1,0:T(8,128)} async-done(((f32[768,768]{1,0:T(8,128)}), f32[24,768]{1,0:T(8,128)}) %reduce-scatter.25.cloned.1.call-update) | async-done | bytes 73744 | tf_op jit(solution)/shard_map/reduce_scatter | solution.py:414
  1522.9 103.8 %reduce-scatter.21.cloned.1.call-done = f32[24,768]{1,0:T(8,128)} async-done(((f32[768,768]{1,0:T(8,128)}), f32[24,768]{1,0:T(8,128)}) %reduce-scatter.21.cloned.1.call-update) | async-done | bytes 73744 | tf_op jit(solution)/shard_map/reduce_scatter | solution.py:412
  1626.7 104.6 %reduce-scatter.23.cloned.1.call-done = f32[24,768]{1,0:T(8,128)} async-done(((f32[768,768]{1,0:T(8,128)}), f32[24,768]{1,0:T(8,128)}) %reduce-scatter.23.cloned.1.call-update) | async-done | bytes 73744 | tf_op jit(solution)/shard_map/reduce_scatter | solution.py:413
  1731.3 141.2 %reduce-scatter.27.cloned.1.call-done = f32[24,3072]{1,0:T(8,128)} async-done(((f32[768,3072]{1,0:T(8,128)}), f32[24,3072]{1,0:T(8,128)}) %reduce-scatter.27.cloned.1.call-update) | async-done | bytes 294928 | tf_op jit(solution)/shard_map/reduce_scatter | solution.py:415
  1872.5 141.8 %reduce-scatter.29.cloned.1.call-done = f32[96,768]{1,0:T(8,128)} async-done(((f32[3072,768]{1,0:T(8,128)}), f32[96,768]{1,0:T(8,128)}) %reduce-scatter.29.cloned.1.call-update) | async-done | bytes 294928 | tf_op jit(solution)/shard_map/reduce_scatter | solution.py:416
  (739 shorter events, 995.6 us)
Async XLA Ops:
  7.2 76.2 %all-gather.11.cloned.1.call-start = ((), (), s32[]{:S(2)}) async-start(), calls=%async_computation.14 | async-start | bytes 1216512 | tf_op jit(solution)/shard_map/all_gather | solution.py:249
  7.9 123.0 %all-gather.15.cloned.1.call-start = ((), (), s32[]{:S(2)}) async-start(), calls=%async_computation.16 | async-start | bytes 1216512 | tf_op jit(solution)/shard_map/all_gather | solution.py:248
  14.1 23.0 %all-to-all-start = ((bf16[4,96,768]{2,1,0:T(8,128)(2,1)}), bf16[4,96,768]{2,1,0:T(8,128)(2,1)S(1)}, u32[]{:S(2)}, u32[]{:S(2)}) async-start(bf16[4,96,768]{2,1,0:T(8,128)(2,1)} %bitcast.1), calls=%async_computation | async-start | bytes 1179648 | tf_op jit(solution)/shard_map/all_to_all | solution.py:270
  20.4 166.5 %all-gather.19.cloned.1.call-start = ((), (), s32[]{:S(2)}) async-start(), calls=%async_computation.18 | async-start | bytes 1216512 | tf_op jit(solution)/shard_map/all_gather | solution.py:247
  37.1 45.5 %all-to-all-start.1 = ((bf16[4,96,768]{2,1,0:T(8,128)(2,1)}), bf16[4,96,768]{2,1,0:T(8,128)(2,1)S(1)}, u32[]{:S(2)}, u32[]{:S(2)}) async-start(bf16[4,96,768]{2,1,0:T(8,128)(2,1)} %bitcast.10), calls=%async_computation.1 | async-start | bytes 1179648 | tf_op jit(solution)/shard_map/all_to_all | solution.py:270
  40.6 197.8 %all-gather.27.cloned.1.call-start = ((), (), s32[]{:S(2)}) async-start(), calls=%async_computation.22 | async-start | bytes 2949120 | tf_op jit(solution)/shard_map/all_gather | solution.py:291
  86.5 203.2 %all-gather.29.cloned.1.call-start = ((), (), s32[]{:S(2)}) async-start(), calls=%async_computation.23 | async-start | bytes 2949120 | tf_op jit(solution)/shard_map/all_gather | solution.py:290
  133.7 400.8 %all-gather.13.cloned.1.call-start = ((), (), s32[]{:S(2)}) async-start(), calls=%async_computation.15 | async-start | bytes 2949120 | tf_op jit(solution)/shard_map/all_gather | solution.py:291
  135.2 414.8 %all-gather.17.cloned.1.call-start = ((), (), s32[]{:S(2)}) async-start(), calls=%async_computation.17 | async-start | bytes 2949120 | tf_op jit(solution)/shard_map/all_gather | solution.py:290
  136.8 659.0 %all-gather.21.cloned.1.call-start = ((), (), s32[]{:S(2)}) async-start(), calls=%async_computation.19 | async-start | bytes 1216512 | tf_op jit(solution)/shard_map/all_gather | solution.py:250
  137.6 663.4 %all-gather.23.cloned.1.call-start = ((), (), s32[]{:S(2)}) async-start(), calls=%async_computation.20 | async-start | bytes 4866048 | tf_op jit(solution)/shard_map/all_gather | solution.py:251
  138.3 678.1 %all-gather.25.cloned.1.call-start = ((), (), s32[]{:S(2)}) async-start(), calls=%async_computation.21 | async-start | bytes 4866048 | tf_op jit(solution)/shard_map/all_gather | solution.py:252
  138.9 1067.2 %reduce-scatter.31.cloned.1.call-start = ((), (), s32[]{:S(2)}) async-start(), calls=%async_computation.30 | async-start | bytes 2949120
  1017.1 192.6 %reduce-scatter.35.cloned.1.call-start = ((), (), s32[]{:S(2)}) async-start(), calls=%async_computation.32 | async-start | bytes 2949120
  1161.3 96.7 %reduce-scatter.33.cloned.1.call-start = ((), (), s32[]{:S(2)}) async-start(), calls=%async_computation.31 | async-start | bytes 2949120
  1177.9 129.7 %reduce-scatter.37.cloned.1.call-start = ((), (), s32[]{:S(2)}) async-start(), calls=%async_computation.33 | async-start | bytes 2949120
  1194.7 235.6 %reduce-scatter.19.cloned.1.call-start = ((), (), s32[]{:S(2)}) async-start(), calls=%async_computation.24 | async-start | bytes 2433024 | tf_op jit(solution)/shard_map/reduce_scatter | solution.py:411
  1200.6 322.3 %reduce-scatter.25.cloned.1.call-start = ((), (), s32[]{:S(2)}) async-start(), calls=%async_computation.27 | async-start | bytes 2433024 | tf_op jit(solution)/shard_map/reduce_scatter | solution.py:414
  1206.1 420.6 %reduce-scatter.21.cloned.1.call-start = ((), (), s32[]{:S(2)}) async-start(), calls=%async_computation.25 | async-start | bytes 2433024 | tf_op jit(solution)/shard_map/reduce_scatter | solution.py:412
  1214.0 517.3 %reduce-scatter.23.cloned.1.call-start = ((), (), s32[]{:S(2)}) async-start(), calls=%async_computation.26 | async-start | bytes 2433024 | tf_op jit(solution)/shard_map/reduce_scatter | solution.py:413
  1311.9 560.6 %reduce-scatter.27.cloned.1.call-start = ((), (), s32[]{:S(2)}) async-start(), calls=%async_computation.28 | async-start | bytes 9732096 | tf_op jit(solution)/shard_map/reduce_scatter | solution.py:415
  1322.9 691.4 %reduce-scatter.29.cloned.1.call-start = ((), (), s32[]{:S(2)}) async-start(), calls=%async_computation.29 | async-start | bytes 9732096 | tf_op jit(solution)/shard_map/reduce_scatter | solution.py:416
  1343.1 19.6 all-to-all-start.3
  1363.6 62.4 %all-to-all-start.2 = ((bf16[4,96,768]{2,1,0:T(8,128)(2,1)}), bf16[4,96,768]{2,1,0:T(8,128)(2,1)}, u32[]{:S(2)}, u32[]{:S(2)}) async-start(bf16[4,96,768]{2,1,0:T(8,128)(2,1)} %bitcast.574), calls=%async_computation.2 | async-start | bytes 1179648 | tf_op jit(solution)/shard_map/all_to_all | solution.py:402
  (179 other events, 1654.2 us)
Sparse Core Ops, SparseCore 0:
  10.8 64.3 all-gather.10
  78.0 52.8 all-gather.14
  133.8 53.0 all-gather.18
  188.9 49.4 all-gather.26
  240.3 49.2 all-gather.28
  291.1 49.2 all-gather.12
  342.0 49.2 all-gather.16
  394.1 52.8 all-gather.20
  449.8 62.4 all-gather.22
  515.0 62.3 all-gather.24
  1017.2 46.7 reduce-scatter.30
  1161.4 46.6 reduce-scatter.34
  1210.3 47.5 reduce-scatter.32
  1260.1 47.5 reduce-scatter.36
  1313.3 104.9 reduce-scatter.18
  1424.9 97.9 reduce-scatter.24
  1528.6 98.0 reduce-scatter.20
  1633.2 98.0 reduce-scatter.22
  1737.8 134.6 reduce-scatter.26
  1879.8 134.4 reduce-scatter.28
where the time goes:
time: 2030 us; the launch traced here: 2020 us
  waiting for transfers between devices  875 us (43%)
  matrix products  600 us (30%)
  local copies, waits for them, and re-layouts  325 us (16%)
  other arithmetic  88.1 us (4%)
  blocking collectives  81.9 us (4%)
    dot_general x18, matrix products, block_scores(): jnp.einsum('qkb,bh->hqk', bucket_hit, rel_bucket, precision=lax.Precision...  206 us
    dot_general x12, local copies, waits for them, and re-layouts, block_scores(): jnp.einsum('qkb,bh->hqk', bucket_hit, rel_bucket, precision=lax.Precision...  143 us
    reduce_scatter x1, waiting for transfers between devices, on_device(): lax.psum_scatter(acc_outer, ('dp', 'fsdp'), scatter_dimension=0, tiled=True)  142 us
    reduce_scatter x1, waiting for transfers between devices, on_device(): lax.psum_scatter(acc_inner, ('dp', 'fsdp'), scatter_dimension=0, tiled=True)  141 us
    unnamed x242, local copies, waits for them, and re-layouts  107 us
    reduce_scatter x1, waiting for transfers between devices, on_device(): lax.psum_scatter(acc_value, ('dp', 'fsdp'), scatter_dimension=0, tiled=True)  105 us
    reduce_scatter x1, waiting for transfers between devices, on_device(): lax.psum_scatter(acc_key, ('dp', 'fsdp'), scatter_dimension=0, tiled=True)  104 us
    unnamed x24, waiting for transfers between devices  94.4 us
  transfers between devices with their start and end apart: 24, of which 13 were waited for; matrix products, arithmetic and copies ran while one was open for 40% of the time, Pallas kernels for 0%

commit v1 on v0

--- a/solution.py
+++ b/solution.py
@@ -1,16 +1,722 @@
+import functools
 import math
 
 import jax
 import jax.numpy as jnp
 from jax import lax
+from jax.experimental import pallas as pl
+from jax.experimental.pallas import tpu as pltpu
 from jax.sharding import PartitionSpec as P
 
 H = 12
 BUCKETS = 32
-
-
 EPSILON = 1e-06
 NEG_FILL = -1e30
+MESH = pl.DeviceIdType.MESH
+TILE = 128
+PAIRS = 6
+OWN = 6
+TILES = 12
+FAR = 6
+SEQS = 4
+
+
+def lane_index(shape):
+    return lax.broadcasted_iota(jnp.int32, shape, len(shape) - 1)
+
+
+def row_index(shape):
+    return lax.broadcasted_iota(jnp.int32, shape, len(shape) - 2)
+
+
+def dot_nn(left, right):
+    return lax.dot_general(left, right, (((1,), (0,)), ((), ())), preferred_element_type=jnp.float32)
+
+
+def dot_nt(left, right):
+    return lax.dot_general(left, right, (((1,), (1,)), ((), ())), preferred_element_type=jnp.float32)
+
+
+def dot_tn(left, right):
+    return lax.dot_general(left, right, (((0,), (0,)), ((), ())), preferred_element_type=jnp.float32)
+
+
+def segments_of(places, lens_ref, count):
+    edge = jnp.int32(0)
+    found = jnp.zeros(places.shape, jnp.int32)
+    for s in range(count - 1):
+        edge = edge + lens_ref[0, s]
+        found = found + (places >= edge).astype(jnp.int32)
+    return found
+
+
+def segment_tags(places, lens_ref, count, of_key):
+    lane = lane_index(places.shape)
+    hit = segments_of(places, lens_ref, count) == lane
+    if of_key:
+        return jnp.where((lane < count) & jnp.logical_not(hit), NEG_FILL, 0.0).astype(jnp.bfloat16)
+    return jnp.where(hit, 1.0, 0.0).astype(jnp.bfloat16)
+
+
+def key_range(i):
+    return max(0, 2 * i - FAR), min(TILES, 2 * i + FAR + 2)
+
+
+def fill_bias(rows_ref, tiles_ref, heads):
+    def one_head(h, carry):
+        for cls in range(3):
+            row = rows_ref[cls, h]
+            wide = pltpu.roll(
+                jnp.broadcast_to(row, (TILE, 2 * TILE)), 0, 1, stride=1, stride_axis=0
+            )
+            tiles_ref[h, cls + 1] = wide[:, :TILE]
+        left = rows_ref[3, h, :, :TILE]
+        right = rows_ref[4, h, :, :TILE]
+        tiles_ref[h, 0] = jnp.broadcast_to(left, (TILE, TILE))
+        tiles_ref[h, 4] = jnp.broadcast_to(right, (TILE, TILE))
+        return carry
+
+    lax.fori_loop(0, heads, one_head, 0)
+
+
+def bias_class(kt, i, core):
+    return jnp.clip(kt - 2 * i - core, -2, 2) + 2
+
+
+def attn_fwd(
+    lens_ref, x_ref, gain_ref, wq_ref, wk_ref, wv_ref, rows_ref,
+    q_ref, k_ref, v_ref, o_ref, log_ref,
+    bias_ref, ext_q, ext_k, s_ref, log_acc, send_sem, recv_sem,
+):
+    dp, z = lax.axis_index("dp"), lax.axis_index("fsdp")
+    core = lax.rem(dp, 2)
+    other = dp + 1 - 2 * core
+    barrier = pltpu.get_barrier_semaphore()
+    pl.semaphore_signal(barrier, inc=1, device_id=(other, z), device_id_type=MESH)
+
+    rows = x_ref[...].astype(jnp.float32)
+    scale = lax.rsqrt(jnp.mean(rows * rows, axis=1, keepdims=True) + EPSILON)
+    normed = (rows * scale * gain_ref[0:1, :]).astype(jnp.bfloat16)
+
+    def project(w_ref):
+        return dot_nn(normed, w_ref[...]).astype(jnp.bfloat16)
+
+    copies = []
+    for n, (w_ref, all_ref) in enumerate(((wk_ref, k_ref), (wv_ref, v_ref))):
+        made = project(w_ref)
+        for hp in range(PAIRS):
+            for i in range(OWN):
+                all_ref[hp, i, core] = made[TILE * i : TILE * (i + 1), 128 * hp : 128 * (hp + 1)]
+        if n == 0:
+            pl.semaphore_wait(barrier, 1)
+        copy = pltpu.make_async_remote_copy(
+            all_ref.at[:, :, core], all_ref.at[:, :, core], send_sem.at[n], recv_sem.at[n],
+            device_id=(other, z), device_id_type=MESH,
+        )
+        copy.start()
+        copies.append(copy)
+    made = project(wq_ref)
+    for hp in range(PAIRS):
+        for i in range(OWN):
+            q_ref[hp, i] = made[TILE * i : TILE * (i + 1), 128 * hp : 128 * (hp + 1)]
+    count = SEQS
+    for t in range(TILES):
+        ext_k[t] = segment_tags(TILE * t + row_index((TILE, 128)), lens_ref, count, True)
+    for i in range(OWN):
+        ext_q[i] = segment_tags(TILE * (2 * i + core) + row_index((TILE, 128)), lens_ref, count, False)
+        log_acc[i] = jnp.zeros((TILE, 128), jnp.float32)
+    fill_bias(rows_ref, bias_ref, 2 * PAIRS)
+    for n, all_ref in enumerate((k_ref, v_ref)):
+        pltpu.make_async_remote_copy(
+            all_ref.at[:, :, 1 - core], all_ref.at[:, :, 1 - core], send_sem.at[n], recv_sem.at[n],
+            device_id=(other, z), device_id_type=MESH,
+        ).wait_recv()
+
+    lane = lane_index((TILE, 128))
+
+    def one_pair(hp, carry):
+        for i in range(OWN):
+            lo, hi = key_range(i)
+            width = (hi - lo) * TILE
+            pair = q_ref[hp, i]
+            tags = ext_q[i]
+            zero = jnp.zeros_like(pair)
+            left = jnp.concatenate(
+                [
+                    jnp.concatenate([jnp.where(lane < 64, pair, zero), tags], axis=1),
+                    jnp.concatenate([jnp.where(lane < 64, zero, pair), tags], axis=1),
+                ],
+                axis=0,
+            )
+            keys = k_ref[hp, lo // 2 : hi // 2].reshape(width, 128)
+            right = jnp.concatenate([keys, ext_k[lo:hi].reshape(width, 128)], axis=1)
+            raw = dot_nt(left, right)
+            tops = []
+            for e in range(2):
+                top = None
+                for kt in range(lo, hi):
+                    at = (kt - lo) * TILE
+                    part = raw[e * TILE : (e + 1) * TILE, at : at + TILE]
+                    if -1 <= kt - 2 * i <= 2:
+                        part = part + bias_ref[2 * hp + e, bias_class(kt, i, core)]
+                    else:
+                        part = part + rows_ref[3 if kt < 2 * i else 4, 2 * hp + e, :, :TILE]
+                    s_ref[e, :, at : at + TILE] = part
+                    top = part if top is None else jnp.maximum(top, part)
+                tops.append(jnp.max(top, axis=1, keepdims=True))
+            outs = []
+            for e in range(2):
+                total = None
+                pieces = []
+                for kt in range(lo, hi):
+                    at = (kt - lo) * TILE
+                    weight = jnp.exp(s_ref[e, :, at : at + TILE] - tops[e])
+                    total = weight if total is None else total + weight
+                    pieces.append(weight.astype(jnp.bfloat16))
+                total = jnp.sum(total, axis=1, keepdims=True)
+                probs = jnp.concatenate(pieces, axis=1)
+                values = v_ref[hp, lo // 2 : hi // 2].reshape(width, 128)
+                outs.append(dot_nn(probs, values) / total)
+                log_acc[i] = jnp.where(lane == 2 * hp + e, tops[e] + jnp.log(total), log_acc[i])
+            o_ref[hp, i] = jnp.where(lane < 64, outs[0], outs[1])
+        return carry
+
+    lax.fori_loop(0, PAIRS, one_pair, 0)
+    for i in range(OWN):
+        turned = log_acc[i].T
+        for h in range(2 * PAIRS):
+            log_ref[i, h] = turned[h : h + 1, :]
+    for copy in copies:
+        copy.wait_send()
+
+
+def attn_bwd(
+    lens_ref, q_ref, k_ref, v_ref, log_ref, do_ref, delta_ref, rows_ref,
+    dq_ref, dk_ref, dv_ref, hist_ref,
+    bias_ref, acc_ref, ext_q, ext_k, dk_acc, dv_acc, out_k, out_v, got_k, got_v, send_sem, recv_sem,
+):
+    dp, z = lax.axis_index("dp"), lax.axis_index("fsdp")
+    core = lax.rem(dp, 2)
+    other = dp + 1 - 2 * core
+    barrier = pltpu.get_barrier_semaphore()
+    pl.semaphore_signal(barrier, inc=1, device_id=(other, z), device_id_type=MESH)
+    count = SEQS
+    for t in range(TILES):
+        ext_k[t] = segment_tags(TILE * t + row_index((TILE, 128)), lens_ref, count, True)
+    for i in range(OWN):
+        ext_q[i] = segment_tags(TILE * (2 * i + core) + row_index((TILE, 128)), lens_ref, count, False)
+    fill_bias(rows_ref, bias_ref, 2 * PAIRS)
+    acc_ref[...] = jnp.zeros_like(acc_ref)
+    pl.semaphore_wait(barrier, 1)
+    lane = lane_index((TILE, 128))
+
+    def one_pair(hp, carry):
+        dk_acc[...] = jnp.zeros_like(dk_acc)
+        dv_acc[...] = jnp.zeros_like(dv_acc)
+        for i in range(OWN):
+            lo, hi = key_range(i)
+            width = (hi - lo) * TILE
+            pair, d_pair = q_ref[hp, i], do_ref[hp, i]
+            tags = ext_q[i]
+            zero = jnp.zeros_like(pair)
+            q_two = jnp.concatenate([jnp.where(lane < 64, pair, zero), jnp.where(lane < 64, zero, pair)], axis=0)
+            d_two = jnp.concatenate([jnp.where(lane < 64, d_pair, zero), jnp.where(lane < 64, zero, d_pair)], axis=0)
+            q_ext = jnp.concatenate([q_two, jnp.concatenate([tags, tags], axis=0)], axis=1)
+            keys = k_ref[hp, lo // 2 : hi // 2].reshape(width, 128)
+            values = v_ref[hp, lo // 2 : hi // 2].reshape(width, 128)
+            k_ext = jnp.concatenate([keys, ext_k[lo:hi].reshape(width, 128)], axis=1)
+            raw = dot_nt(k_ext, q_ext)
+            d_probs = dot_nt(values, d_two)
+            p_rows, s_rows = [], []
+            for kt in range(lo, hi):
+                at = (kt - lo) * TILE
+                p_two, s_two = [], []
+                for e in range(2):
+                    head = 2 * hp + e
+                    part = raw[at : at + TILE, e * TILE : (e + 1) * TILE]
+                    near = -1 <= kt - 2 * i <= 2
+                    cls = bias_class(kt, i, core) if near else (0 if kt < 2 * i else 4)
+                    if near:
+                        part = part + bias_ref[head, cls]
+                    else:
+                        part = part + rows_ref[3 if kt < 2 * i else 4, head, :, :TILE]
+                    probs = jnp.exp(part - log_ref[i, head])
+                    slope = probs * (
+                        d_probs[at : at + TILE, e * TILE : (e + 1) * TILE] - delta_ref[i, head]
+                    )
+                    acc_ref[head, cls] += slope
+                    p_two.append(probs.astype(jnp.bfloat16))
+                    s_two.append(slope.astype(jnp.bfloat16))
+                p_rows.append(jnp.concatenate(p_two, axis=1))
+                s_rows.append(jnp.concatenate(s_two, axis=1))
+            probs_t = jnp.concatenate(p_rows, axis=0)
+            slopes_t = jnp.concatenate(s_rows, axis=0)
+            dv_acc[lo * TILE : hi * TILE, :] += dot_nn(probs_t, d_two)
+            dk_acc[lo * TILE : hi * TILE, :] += dot_nn(slopes_t, q_two)
+            d_q = dot_tn(slopes_t, keys)
+            dq_ref[hp, i] = jnp.where(lane < 64, d_q[:TILE], d_q[TILE:]).astype(jnp.bfloat16)
+        for acc, own, out in ((dk_acc, dk_ref, out_k), (dv_acc, dv_ref, out_v)):
+            for i in range(OWN):
+                own[hp, i] = acc[pl.ds((2 * i + core) * TILE, TILE), :].astype(jnp.bfloat16)
+                out[hp, i] = acc[pl.ds((2 * i + 1 - core) * TILE, TILE), :].astype(jnp.bfloat16)
+        for n, (out, got) in enumerate(((out_k, got_k), (out_v, got_v))):
+            pltpu.make_async_remote_copy(
+                out.at[hp], got.at[hp], send_sem.at[n, hp], recv_sem.at[n, hp],
+                device_id=(other, z), device_id_type=MESH,
+            ).start()
+        return carry
+
+    lax.fori_loop(0, PAIRS, one_pair, 0)
+    flip = (row_index((TILE, TILE)) + lane == TILE - 1).astype(jnp.float32)
+
+    def one_head(h, carry):
+        for cls in range(3):
+            tile = jnp.dot(flip, acc_ref[h, cls + 1], precision=lax.Precision.HIGHEST)
+            wide = jnp.concatenate([tile, jnp.zeros((TILE, TILE), jnp.float32)], axis=1)
+            wide = pltpu.roll(wide, 0, 1, stride=1, stride_axis=0)
+            hist_ref[cls, h] = jnp.sum(wide, axis=0, keepdims=True)
+        for n, cls in ((3, 0), (4, 4)):
+            row = jnp.sum(acc_ref[h, cls], axis=0, keepdims=True)
+            hist_ref[n, h] = jnp.concatenate([row, jnp.zeros_like(row)], axis=1)
+        return carry
+
+    lax.fori_loop(0, 2 * PAIRS, one_head, 0)
+
+    def finish(hp, carry):
+        for n, (out, got, own) in enumerate(((out_k, got_k, dk_ref), (out_v, got_v, dv_ref))):
+            copy = pltpu.make_async_remote_copy(
+                out.at[hp], got.at[hp], send_sem.at[n, hp], recv_sem.at[n, hp],
+                device_id=(other, z), device_id_type=MESH,
+            )
+            copy.wait_send()
+            copy.wait_recv()
+            own[hp] = (own[hp].astype(jnp.float32) + got[hp].astype(jnp.float32)).astype(jnp.bfloat16)
+        return carry
+
+    lax.fori_loop(0, PAIRS, finish, 0)
+
+
+def norm_back(rows_in, scale, gain, grad_normed):
+    scaled = grad_normed * gain
+    grad_gain = jnp.sum(grad_normed * rows_in * scale, axis=0, keepdims=True)
+    shared = jnp.mean(scaled * rows_in, axis=1, keepdims=True)
+    return scale * scaled - rows_in * (scale * scale * scale * shared), grad_gain
+
+
+def join_pairs(pairs_ref, joined_ref):
+    for hp in range(PAIRS):
+        joined_ref[:, 128 * hp : 128 * (hp + 1)] = (
+            pairs_ref[hp].reshape(OWN * TILE, 128).astype(joined_ref.dtype)
+        )
+
+
+def ffn_kernel(
+    deal_ref, x_ref, o_ref, g_ref, wo_ref, gain_ref, wi_ref, wu_ref,
+    out_ref, dmid_ref, datt_ref, delta_ref, gwo_ref, gwi_ref, gwu_ref, ggain_ref,
+    att_ref, grad_ref, mid_ref, normed_ref, total_ref, back_ref,
+):
+    step = pl.program_id(0)
+    tok = OWN * TILE
+
+    @pl.when(step == 0)
+    def _():
+        core = lax.rem(lax.axis_index("dp"), 2)
+        for i in range(OWN):
+            places = (2 * i + core) * TILE + row_index((TILE, TILES * TILE))
+            pick = jnp.where(deal_ref[...] == places, 1.0, 0.0).astype(jnp.bfloat16)
+            grad_ref[TILE * i : TILE * (i + 1), :] = dot_nn(pick, g_ref[...]).astype(jnp.bfloat16)
+        join_pairs(o_ref, att_ref)
+        mid = x_ref[...].astype(jnp.float32) + dot_nn(att_ref[...], wo_ref[...])
+        mid_ref[...] = mid
+        scale = lax.rsqrt(jnp.mean(mid * mid, axis=1, keepdims=True) + EPSILON)
+        normed_ref[...] = (mid * scale * gain_ref[0:1, :]).astype(jnp.bfloat16)
+        total_ref[...] = jnp.zeros_like(total_ref)
+        back_ref[...] = jnp.zeros_like(back_ref)
+
+    normed = normed_ref[...]
+    grad = grad_ref[...]
+    inner = dot_nn(normed, wi_ref[...])
+    cdf = 0.5 * (1.0 + lax.erf(inner * (1.0 / math.sqrt(2.0))))
+    active = (inner * cdf).astype(jnp.bfloat16)
+    slope = cdf + inner * (jnp.exp(-0.5 * inner * inner) * (1.0 / math.sqrt(2.0 * math.pi)))
+    total_ref[...] += dot_nn(active, wu_ref[...])
+    d_inner = (dot_nt(grad, wu_ref[...]) * slope).astype(jnp.bfloat16)
+    gwu_ref[...] = dot_tn(active, grad).astype(gwu_ref.dtype)
+    gwi_ref[...] = dot_tn(normed, d_inner).astype(gwi_ref.dtype)
+    back_ref[...] += dot_nt(d_inner, wi_ref[...])
+
+    @pl.when(step == pl.num_programs(0) - 1)
+    def _():
+        mid = mid_ref[...]
+        out_ref[...] = (mid + total_ref[...]).astype(out_ref.dtype)
+        scale = lax.rsqrt(jnp.mean(mid * mid, axis=1, keepdims=True) + EPSILON)
+        d_rows, d_gain = norm_back(mid, scale, gain_ref[0:1, :], back_ref[...])
+        ggain_ref[...] = jnp.broadcast_to(d_gain, ggain_ref.shape)
+        d_mid = grad_ref[...].astype(jnp.float32) + d_rows
+        dmid_ref[...] = d_mid
+        branch = d_mid.astype(jnp.bfloat16)
+        gwo_ref[...] = dot_tn(att_ref[...], branch).astype(gwo_ref.dtype)
+        d_att = dot_nt(branch, wo_ref[...]).astype(jnp.bfloat16)
+        pick = (lane_index((16, PAIRS * 128)) // 64 == row_index((16, PAIRS * 128))).astype(jnp.float32)
+        sums = None
+        for hp in range(PAIRS):
+            part = d_att[:, 128 * hp : 128 * (hp + 1)]
+            datt_ref[hp] = part.reshape(OWN, TILE, 128)
+            prod = part.astype(jnp.float32) * o_ref[hp].reshape(tok, 128)
+            term = lax.dot_general(
+                pick[:, 128 * hp : 128 * (hp + 1)], prod, (((1,), (1,)), ((), ())),
+                precision=lax.Precision.HIGHEST, preferred_element_type=jnp.float32,
+            )
+            sums = term if sums is None else sums + term
+        for i in range(OWN):
+            for h in range(2 * PAIRS):
+                delta_ref[i, h] = sums[h : h + 1, TILE * i : TILE * (i + 1)]
+
+
+def qkv_back_kernel(
+    x_ref, gain_ref, dmid_ref, dq_ref, dk_ref, dv_ref, wq_ref, wk_ref, wv_ref,
+    gq_ref, gk_ref, gv_ref, ddealt_ref, ggain_ref, join_ref,
+):
+    rows = x_ref[...].astype(jnp.float32)
+    scale = lax.rsqrt(jnp.mean(rows * rows, axis=1, keepdims=True) + EPSILON)
+    normed_t = (rows * scale * gain_ref[0:1, :]).astype(jnp.bfloat16).T
+    back = None
+    for pairs, w_ref, g_ref in ((dq_ref, wq_ref, gq_ref), (dk_ref, wk_ref, gk_ref), (dv_ref, wv_ref, gv_ref)):
+        join_pairs(pairs, join_ref)
+        grad = join_ref[...]
+        g_ref[...] = dot_nn(normed_t, grad).astype(g_ref.dtype)
+        term = dot_nt(grad, w_ref[...])
+        back = term if back is None else back + term
+    d_rows, d_gain = norm_back(rows, scale, gain_ref[0:1, :], back)
+    ggain_ref[...] = jnp.broadcast_to(d_gain, ggain_ref.shape)
+    ddealt_ref[...] = (dmid_ref[...] + d_rows).astype(ddealt_ref.dtype)
+
+
+def coordinates():
+    dp, z = lax.axis_index("dp"), lax.axis_index("fsdp")
+    return dp // 4, lax.rem(dp // 2, 2), lax.rem(dp, 2), z
+
+
+def place(y, x, c, z):
+    return (4 * y + 2 * x + c, z)
+
+
+def column(y, x, c):
+    return 16 * y + 8 * x + 4 * c
+
+
+def greet(barrier):
+    y, x, c, z = coordinates()
+    partners = [place(1 - y, x, c, z), place(y, 1 - x, c, z)]
+    for dc in range(2):
+        for dz in range(4):
+            if dc or dz:
+                partners.append(place(y, x, lax.rem(c + dc, 2), lax.rem(z + dz, 4)))
+    for partner in partners:
+        pl.semaphore_signal(barrier, inc=1, device_id=partner, device_id_type=MESH)
+    pl.semaphore_wait(barrier, len(partners))
+
+
+def remote(src, dst, send, recv, target):
+    return pltpu.make_async_remote_copy(
+        src, dst, send, recv, device_id=target, device_id_type=MESH
+    )
+
+
+def send_or_keep(src, dst, send, recv, target, here):
+    @pl.when(jnp.logical_not(here))
+    def _():
+        remote(src, dst, send, recv, target).start()
+
+    @pl.when(here)
+    def _():
+        pltpu.make_async_copy(src, dst, recv).start()
+
+
+def sent(src, dst, send, recv, target, here):
+    @pl.when(jnp.logical_not(here))
+    def _():
+        remote(src, dst, send, recv, target).wait_send()
+
+
+def gather_kernel(first_axis, *refs):
+    count = len(first_axis)
+    lens_in, deal_in, hid_in, grd_in = refs[:4]
+    shards = refs[4 : 4 + count]
+    lens_u, deal_u, x_own, g_all = refs[4 + count : 8 + count]
+    outs = refs[8 + count : 8 + 2 * count]
+    w_send, w_recv, w_local, x_send, x_recv, g_send, g_recv, p_send, p_recv = refs[8 + 2 * count :]
+    y, x, c, z = coordinates()
+    sibling = place(y, x, 1 - c, z)
+    greet(pltpu.get_barrier_semaphore())
+
+    def token_sends():
+        for m in range(2):
+            for l in range(3):
+                t = 3 * z + l
+                core_to, z_to = lax.rem(t, 2), 2 * c + m
+                yield (
+                    hid_in.at[m, l], x_own.at[t // 2], x_send.at[m, l], x_recv.at[t // 2],
+                    place(y, x, core_to, z_to), (core_to == c) & (z_to == z),
+                )
+
+    def grad_sends():
+        for m in range(2):
+            for half in range(2):
+                z_to = 2 * c + m
+                yield (
+                    grd_in.at[m, half], g_all.at[2 * z + half], g_send.at[0, m, half], g_recv.at[0, z],
+                    place(y, x, half, z_to), (half == c) & (z_to == z),
+                )
+
+    for item in token_sends():
+        send_or_keep(*item)
+    owner, micro = z // 2, lax.rem(z, 2)
+    plans = []
+    for n, (src, dst) in enumerate(((lens_in, lens_u), (deal_in, deal_u))):
+        plans.append((src.at[micro], dst, p_send.at[n], p_recv.at[n]))
+
+    @pl.when(owner == c)
+    def _():
+        for src, dst, send, recv in plans:
+            remote(src, dst, send, recv, sibling).start()
+            pltpu.make_async_copy(src, dst, recv).start()
+
+    own = column(y, x, c) + z
+
+    def start(w):
+        pltpu.make_async_copy(shards[w], outs[w].at[own], w_local.at[w]).start()
+        for dz in range(1, 4):
+            remote(
+                shards[w], outs[w].at[own], w_send.at[w, dz - 1], w_recv.at[w, dz - 1],
+                place(y, x, c, lax.rem(z + dz, 4)),
+            ).start()
+
+    def sides(w):
+        if first_axis[w] == "x":
+            return place(y, 1 - x, c, z), place(1 - y, x, c, z), column(y, 1 - x, c), column(1 - y, x, c)
+        return place(1 - y, x, c, z), place(y, 1 - x, c, z), column(1 - y, x, c), column(y, 1 - x, c)
+
+    def push(w, k, base, target):
+        block = outs[w].at[pl.ds(base, 4)]
+        return remote(block, block, w_send.at[w, k], w_recv.at[w, k], target)
+
+    far_column = column(1 - y, 1 - x, c)
+
+    def spread_own(w):
+        near, side, _, _ = sides(w)
+        pltpu.make_async_copy(shards[w], outs[w].at[own], w_local.at[w]).wait()
+        for dz in range(1, 4):
+            came = column(y, x, c) + lax.rem(z + 4 - dz, 4)
+            remote(
+                shards[w], outs[w].at[came], w_send.at[w, dz - 1], w_recv.at[w, dz - 1], sibling
+            ).wait_recv()
+        mine = column(y, x, c)
+        for k, target in ((3, near), (4, side), (6, sibling)):
+            push(w, k, mine, target).start()
+
+    def spread_near(w):
+        _, side, near_column, _ = sides(w)
+        push(w, 3, near_column, sibling).wait_recv()
+        push(w, 5, near_column, side).start()
+        push(w, 7, near_column, sibling).start()
+
+    def spread_side(w):
+        _, _, _, side_column = sides(w)
+        push(w, 4, side_column, sibling).wait_recv()
+        push(w, 8, side_column, sibling).start()
+        push(w, 5, far_column, sibling).wait_recv()
+        push(w, 9, far_column, sibling).start()
+
+    def finish(w):
+        _, _, near_column, side_column = sides(w)
+        for k, base in ((6, column(y, x, c)), (7, near_column), (8, side_column), (9, far_column)):
+            push(w, k, base + 4 - 8 * c, sibling).wait_recv()
+        for dz in range(1, 4):
+            remote(
+                shards[w], outs[w].at[own], w_send.at[w, dz - 1], w_recv.at[w, dz - 1], sibling
+            ).wait_send()
+        for k in range(3, 10):
+            push(w, k, column(y, x, c), sibling).wait_send()
+
+    ahead = 4
+    for w in range(min(ahead, count)):
+        start(w)
+    for item in grad_sends():
+        send_or_keep(*item)
+    for n in range(count + 3):
+        for back, stage in enumerate((spread_own, spread_near, spread_side, finish)):
+            if 0 <= n - back < count:
+                stage(n - back)
+        if n + ahead < count:
+            start(n + ahead)
+
+    for zs in range(4):
+        block = g_all.at[2 * zs + c]
+        remote(block, block, g_send.at[1, 0, 0], g_recv.at[0, zs], sibling).wait_recv()
+        remote(block, block, g_send.at[1, zs // 2, zs % 2], g_recv.at[1, zs], sibling).start()
+    for item in token_sends():
+        sent(*item)
+    for item in grad_sends():
+        sent(*item)
+    for i in range(OWN):
+        remote(hid_in.at[0, 0], x_own.at[i], x_send.at[0, 0], x_recv.at[i], sibling).wait_recv()
+    for zs in range(4):
+        block = g_all.at[2 * zs + 1 - c]
+        remote(block, block, g_send.at[1, zs // 2, zs % 2], g_recv.at[1, zs], sibling).wait_recv()
+        remote(block, block, g_send.at[1, zs // 2, zs % 2], g_recv.at[1, zs], sibling).wait_send()
+    for src, dst, send, recv in plans:
+        remote(src, dst, send, recv, sibling).wait_recv()
+
+    @pl.when(owner == c)
+    def _():
+        for src, dst, send, recv in plans:
+            remote(src, dst, send, recv, sibling).wait_send()
+
+
+def scatter_kernel(first_axis, *refs):
+    count = len(first_axis)
+    deal_ref, res_in, back_in = refs[:3]
+    grads = refs[3 : 3 + count]
+    hid_out, gin_out = refs[3 + count : 5 + count]
+    outs = refs[5 + count : 5 + 2 * count]
+    scratch = refs[5 + 2 * count :]
+    r1, r2, r3, r4 = (scratch[n * count : (n + 1) * count] for n in range(4))
+    res_all, dealt, w_send, w_recv, b_send, b_recv, h_send, h_recv, e_send, e_recv = scratch[4 * count :]
+    y, x, c, z = coordinates()
+    sibling = place(y, x, 1 - c, z)
+    owner, micro = z // 2, lax.rem(z, 2)
+    greet(pltpu.get_barrier_semaphore())
+
+    def core_copy(w, k):
+        return remote(
+            grads[w].at[pl.ds(8 * k + 4 * (1 - c), 4)], r1[w].at[k], w_send.at[w, k], w_recv.at[w, k], sibling
+        )
+
+    res_copy = remote(res_in, res_all.at[:, c], e_send, e_recv, sibling)
+    res_copy.start()
+
+    def back_sends():
+        for i in range(OWN):
+            t = 2 * i + c
+            z_to, l = t // 3, lax.rem(t, 3)
+            yield (
+                back_in.at[i], gin_out.at[micro, l], b_send.at[i], b_recv.at[micro, l],
+                place(y, x, owner, z_to), (owner == c) & (z_to == z),
+            )
+
+    for item in back_sends():
+        send_or_keep(*item)
+    for w in range(count):
+        for k in range(4):
+            core_copy(w, k).start()
+
+    def sides(w):
+        near, side = place(y, 1 - x, c, z), place(1 - y, x, c, z)
+        index = lambda s, f: 2 * s + f
+        s, f = y, x
+        if first_axis[w] == "y":
+            near, side = side, near
+            index = lambda s, f: 2 * f + s
+            s, f = x, y
+        return near, side, index, s, f
+
+    def add_into(dst, k, src):
+        def one(n, carry):
+            dst[k, n] = dst[k, n] + src[n]
+            return carry
+
+        lax.fori_loop(0, 4, one, 0)
+
+    def side_copy(w, f_at):
+        near, side, index, s, f = sides(w)
+        return remote(
+            r1[w].at[index(1 - s, f_at)], r2[w].at[f_at], w_send.at[w, 4 + f_at], w_recv.at[w, 4 + f_at], side
+        )
+
+    def near_copy(w):
+        near, side, index, s, f = sides(w)
+        return remote(r1[w].at[index(s, 1 - f)], r3[w], w_send.at[w, 6], w_recv.at[w, 6], near)
+
+    def z_copy(w, dz):
+        near, side, index, s, f = sides(w)
+        z_to = lax.rem(z + dz, 4)
+        return remote(
+            r1[w].at[index(s, f), z_to], r4[w].at[dz - 1], w_send.at[w, 6 + dz], w_recv.at[w, 6 + dz],
+            place(y, x, c, z_to),
+        )
+
+    def stage_core(w):
+        for k in range(4):
+            core_copy(w, k).wait_recv()
+            add_into(r1[w], k, grads[w].at[pl.ds(8 * k + 4 * c, 4)])
+        for f_at in range(2):
+            side_copy(w, f_at).start()
+
+    def stage_side(w):
+        near, side, index, s, f = sides(w)
+        for f_at in range(2):
+            side_copy(w, f_at).wait_recv()
+            add_into(r1[w], index(s, f_at), r2[w].at[f_at])
+        near_copy(w).start()
+
+    def stage_near(w):
+        near, side, index, s, f = sides(w)
+        near_copy(w).wait_recv()
+        add_into(r1[w], index(s, f), r3[w])
+        for dz in range(1, 4):
+            z_copy(w, dz).start()
+
+    def stage_z(w):
+        near, side, index, s, f = sides(w)
+        total = r1[w][index(s, f), z].astype(jnp.float32)
+        for dz in range(1, 4):
+            z_copy(w, dz).wait_recv()
+            total = total + r4[w][dz - 1].astype(jnp.float32)
+        outs[w][...] = total
+        for k in range(4):
+            core_copy(w, k).wait_send()
+        for f_at in range(2):
+            side_copy(w, f_at).wait_send()
+        near_copy(w).wait_send()
+        for dz in range(1, 4):
+            z_copy(w, dz).wait_send()
+
+    def dealt_sends():
+        for e in range(2):
+            z_to = 2 * c + e
+            yield (
+                dealt.at[e], hid_out.at[micro], h_send.at[e], h_recv.at[micro],
+                place(y, x, owner, z_to), (owner == c) & (z_to == z),
+            )
+
+    def deal_result():
+        for i in range(OWN):
+            res_all[i, c] = res_in[i]
+        remote(res_in, res_all.at[:, 1 - c], e_send, e_recv, sibling).wait_recv()
+        pick = jnp.where(
+            row_index((TILES * TILE, TILES * TILE // 2)) == deal_ref[c], 1.0, 0.0
+        ).astype(jnp.bfloat16)
+        rows = dot_tn(pick, res_all[...].reshape(TILES * TILE, -1))
+        dealt[...] = rows.astype(jnp.bfloat16).reshape(dealt.shape)
+        for item in dealt_sends():
+            send_or_keep(*item)
+
+    for n in range(count + 3):
+        for back, stage in enumerate((stage_core, stage_side, stage_near, stage_z)):
+            if 0 <= n - back < count:
+                stage(n - back)
+        if n == 0:
+            deal_result()
+    res_copy.wait_send()
+    for item in back_sends():
+        sent(*item)
+    for item in dealt_sends():
+        sent(*item)
+    for m in range(2):
+        remote(dealt.at[0], hid_out.at[m], h_send.at[0], h_recv.at[m], sibling).wait_recv()
+        for l in range(3):
+            remote(back_in.at[0], gin_out.at[m, l], b_send.at[0], b_recv.at[m, l], sibling).wait_recv()
 
 
 def token_places(deal_order, lengths):
@@ -35,7 +741,7 @@
     return normal_cdf + values * normal_pdf
 
 
-def norm_back(rows_in, scale, gain, grad_normed):
+def norm_back_rows(rows_in, scale, gain, grad_normed):
     scaled_grad = grad_normed * gain
     grad_gain = jnp.sum(grad_normed * rows_in * scale, axis=0)
     grad_rows = scale * scaled_grad - rows_in * scale * scale * scale * jnp.mean(
@@ -331,7 +1037,7 @@
         d_normed2 = jnp.einsum(
             "tf,df->td", d_inner, inner_weight, preferred_element_type=jnp.float32
         )
-        d_mid_norm, d_gain_two = norm_back(mid, scale_two, gain_two, d_normed2)
+        d_mid_norm, d_gain_two = norm_back_rows(mid, scale_two, gain_two, d_normed2)
         acc_gain_two = acc_gain_two + d_gain_two
         d_mid = grad_top.astype(jnp.float32) + d_mid_norm
         d_branch = d_mid.astype(jnp.bfloat16)
@@ -396,7 +1102,7 @@
                 "te,de->td", d_values_low, value_weight, preferred_element_type=jnp.float32
             )
         )
-        d_rows_norm, d_gain_one = norm_back(dealt_rows, scale_one, gain_one, d_normed1)
+        d_rows_norm, d_gain_one = norm_back_rows(dealt_rows, scale_one, gain_one, d_normed1)
         acc_gain_one = acc_gain_one + d_gain_one
         d_dealt = d_mid + d_rows_norm
         returned = lax.all_to_all(
@@ -430,39 +1136,262 @@
     )
 
 
+VMEM = pl.BlockSpec(memory_space=pltpu.VMEM)
+SMEM = pl.BlockSpec(memory_space=pltpu.SMEM)
+ANYWHERE = pl.BlockSpec(memory_space=pl.ANY)
+LIMIT = 56 * 1024 * 1024
+FIRST_AXIS = ("x", "x", "y", "x", "y", "x", "y")
+
+
+def shaped(*shape, dtype=jnp.bfloat16):
+    return jax.ShapeDtypeStruct(shape, dtype)
+
+
+def params(collective_id=None):
+    if collective_id is None:
+        return pltpu.CompilerParams(vmem_limit_bytes=LIMIT)
+    return pltpu.CompilerParams(
+        collective_id=collective_id, has_side_effects=True, vmem_limit_bytes=LIMIT
+    )
+
+
+def dma(*shape):
+    return pltpu.SemaphoreType.DMA(shape)
+
+
+def gather_all(lens, deal, hid, grd, shards):
+    count = len(shards)
+    return pl.pallas_call(
+        functools.partial(gather_kernel, FIRST_AXIS),
+        name="gather_all",
+        out_shape=[
+            shaped(*lens.shape[1:], dtype=jnp.int32),
+            shaped(*deal.shape[1:], dtype=jnp.int32),
+            shaped(OWN, TILE, hid.shape[-1]),
+            shaped(8, *grd.shape[2:]),
+        ]
+        + [shaped(32, *s.shape) for s in shards],
+        in_specs=[ANYWHERE] * (4 + count),
+        out_specs=[ANYWHERE] * (4 + count),
+        scratch_shapes=[
+            dma(count, 10), dma(count, 10), dma(count), dma(2, 3), dma(OWN), dma(2, 2, 2), dma(2, 4), dma(2), dma(2),
+        ],
+        compiler_params=params(0),
+    )(lens, deal, hid, grd, *shards)
+
+
+def scatter_all(deal, res, back, grads):
+    count = len(grads)
+    width = res.shape[-1]
+    blocks = [g.shape[1:] for g in grads]
+    return pl.pallas_call(
+        functools.partial(scatter_kernel, FIRST_AXIS),
+        name="scatter_all",
+        out_shape=[shaped(2, 3 * TILE, width), shaped(2, 3, TILE, width)]
+        + [shaped(*b, dtype=jnp.float32) for b in blocks],
+        in_specs=[VMEM] * (3 + count),
+        out_specs=[VMEM] * (2 + count),
+        scratch_shapes=[pltpu.VMEM((4, 4, *b), jnp.bfloat16) for b in blocks]
+        + [pltpu.VMEM((2, 4, *b), jnp.bfloat16) for b in blocks]
+        + [pltpu.VMEM((4, *b), jnp.bfloat16) for b in blocks]
+        + [pltpu.VMEM((3, *b), jnp.bfloat16) for b in blocks]
+        + [
+            pltpu.VMEM((OWN, 2, TILE, width), jnp.bfloat16),
+            pltpu.VMEM((2, 3 * TILE, width), jnp.bfloat16),
+            dma(count, 10), dma(count, 10), dma(OWN), dma(2, 3), dma(2), dma(2),
+            pltpu.SemaphoreType.DMA, pltpu.SemaphoreType.DMA,
+        ],
+        compiler_params=params(3),
+    )(deal, res, back, *grads)
+
+
+def attention_forward(lens, x, gain, wq, wk, wv, rows):
+    heads, keys = (PAIRS, OWN, TILE, 128), (PAIRS, OWN, 2, TILE, 128)
+    return pl.pallas_call(
+        attn_fwd,
+        name="attn_fwd",
+        out_shape=[
+            shaped(*heads), shaped(*keys), shaped(*keys), shaped(*heads, dtype=jnp.float32),
+            shaped(OWN, 2 * PAIRS, 1, TILE, dtype=jnp.float32),
+        ],
+        in_specs=[SMEM] + [VMEM] * 6,
+        out_specs=[VMEM] * 5,
+        scratch_shapes=[
+            pltpu.VMEM((2 * PAIRS, 5, TILE, TILE), jnp.float32),
+            pltpu.VMEM((OWN, TILE, 128), jnp.bfloat16),
+            pltpu.VMEM((TILES, TILE, 128), jnp.bfloat16),
+            pltpu.VMEM((2, TILE, TILES * TILE), jnp.float32),
+            pltpu.VMEM((OWN, TILE, 128), jnp.float32),
+            dma(2), dma(2),
+        ],
+        compiler_params=params(1),
+    )(lens, x, gain, wq, wk, wv, rows)
+
+
+def attention_backward(lens, q, k, v, log_total, d_att, delta, rows):
+    heads = (PAIRS, OWN, TILE, 128)
+    return pl.pallas_call(
+        attn_bwd,
+        name="attn_bwd",
+        out_shape=[shaped(*heads)] * 3 + [shaped(5, 2 * PAIRS, 1, 2 * TILE, dtype=jnp.float32)],
+        in_specs=[SMEM] + [VMEM] * 7,
+        out_specs=[VMEM] * 4,
+        scratch_shapes=[pltpu.VMEM((2 * PAIRS, 5, TILE, TILE), jnp.float32)] * 2
+        + [pltpu.VMEM((OWN, TILE, 128), jnp.bfloat16), pltpu.VMEM((TILES, TILE, 128), jnp.bfloat16)]
+        + [pltpu.VMEM((TILES * TILE, 128), jnp.float32)] * 2
+        + [pltpu.VMEM(heads, jnp.bfloat16)] * 4
+        + [dma(2, PAIRS), dma(2, PAIRS)],
+        compiler_params=params(2),
+    )(lens, q, k, v, log_total, d_att, delta, rows)
+
+
+def feed_forward(deal, x, o, g, wo, gain, wi, wu):
+    tok, width, hidden = x.shape[0], x.shape[1], wi.shape[1]
+    chunk = 512
+    f32 = jnp.float32
+
+    def full(*shape):
+        return pl.BlockSpec(shape, lambda j: (0,) * len(shape))
+
+    columns = pl.BlockSpec((width, chunk), lambda j: (0, j))
+    lines = pl.BlockSpec((chunk, width), lambda j: (j, 0))
+    heads, stats = (PAIRS, OWN, TILE, 128), (OWN, 2 * PAIRS, 1, TILE)
+    return pl.pallas_call(
+        ffn_kernel,
+        name="feed_forward",
+        grid=(hidden // chunk,),
+        out_shape=[
+            shaped(tok, width), shaped(tok, width, dtype=f32), shaped(*heads), shaped(*stats, dtype=f32),
+            shaped(width, width), shaped(width, hidden), shaped(hidden, width), shaped(8, width, dtype=f32),
+        ],
+        in_specs=[
+            full(*deal.shape), full(tok, width), full(*heads), full(2 * tok, width), full(width, width),
+            full(8, width), columns, lines,
+        ],
+        out_specs=[
+            full(tok, width), full(tok, width), full(*heads), full(*stats), full(width, width),
+            columns, lines, full(8, width),
+        ],
+        scratch_shapes=[
+            pltpu.VMEM((tok, width), jnp.bfloat16), pltpu.VMEM((tok, width), jnp.bfloat16),
+            pltpu.VMEM((tok, width), f32), pltpu.VMEM((tok, width), jnp.bfloat16),
+            pltpu.VMEM((tok, width), f32), pltpu.VMEM((tok, width), f32),
+        ],
+        compiler_params=params(),
+    )(deal, x, o, g, wo, gain, wi, wu)
+
+
+def qkv_backward(x, gain, d_mid, dq, dk, dv, wq, wk, wv):
+    tok, width = x.shape
+    return pl.pallas_call(
+        qkv_back_kernel,
+        name="qkv_back",
+        out_shape=[shaped(width, width)] * 3 + [shaped(tok, width), shaped(8, width, dtype=jnp.float32)],
+        in_specs=[VMEM] * 9,
+        out_specs=[VMEM] * 5,
+        scratch_shapes=[pltpu.VMEM((tok, width), jnp.bfloat16)],
+        compiler_params=params(),
+    )(x, gain, d_mid, dq, dk, dv, wq, wk, wv)
+
+
+def bias_rows(rel, turned=False):
+    first, last = rel[:, :1], rel[:, 256:]
+    low, high = rel[:, :128], rel[:, 128:256]
+    spread = lambda one: jnp.broadcast_to(one, low.shape)
+    rows = [
+        jnp.concatenate(pair, axis=1)
+        for pair in (
+            (low, spread(first)), (high, low), (spread(last), high),
+            (spread(first), spread(first)), (spread(last), spread(last)),
+        )
+    ]
+    if turned:
+        rows = [rows[2], rows[1], rows[0], rows[4], rows[3]]
+    return jnp.stack(rows)[:, :, None, :]
+
+
+def on_device_packed(
+    hidden_in, grad_out, gain_attn, gain_ffn, rel_bias,
+    w_query, w_key, w_value, w_output, w_inner, w_outer,
+    dealing, lengths, bucket_table,
+):
+    micro_count, tok_rows, width = hidden_in.shape
+    f32 = jnp.float32
+    line = lambda v: jnp.pad(v, (0, 128 - v.shape[0]))[None]
+    small = jnp.concatenate(
+        [line(gain_attn), line(gain_ffn), line(rel_bias), jnp.zeros((13, 128), jnp.bfloat16)], axis=0
+    )
+    lens = jnp.pad(lengths, ((0, 0), (0, 0), (0, 128 - lengths.shape[2])))
+    gathered = gather_all(
+        lens,
+        dealing,
+        hidden_in.reshape(2, 3, TILE, width),
+        grad_out.reshape(2, 2, tok_rows // 2, width),
+        (small, w_query, w_key, w_value, w_output, w_inner, w_outer),
+    )
+    lens_u, deal_u, x_own, g_all, small_all = gathered[:5]
+    wq, wk, wv, wo, wi, wu = (w.reshape(-1, w.shape[-1]) for w in gathered[5:])
+    gains = [
+        jnp.broadcast_to(small_all[:, n, :24].reshape(1, width).astype(f32), (8, width)) for n in range(2)
+    ]
+    picked = (bucket_table[None, :] == jnp.arange(BUCKETS, dtype=jnp.int32)[:, None]).astype(f32)
+    rel = lax.dot_general(
+        small_all[:, 2, :H].astype(f32), picked, (((0,), (0,)), ((), ())),
+        precision=lax.Precision.HIGHEST, preferred_element_type=f32,
+    )
+    x_rows = x_own.reshape(-1, width)
+    q, k, v, o, log_total = attention_forward(lens_u, x_rows, gains[0], wq, wk, wv, bias_rows(rel))
+    result, d_mid, d_att, delta, g_wo, g_wi, g_wu, g_two = feed_forward(
+        deal_u, x_rows, o, g_all.reshape(-1, width), wo, gains[1], wi, wu
+    )
+    dq, dk, dv, hist = attention_backward(
+        lens_u, q, k, v, log_total, d_att, delta, bias_rows(rel[:, ::-1], True)
+    )
+    g_wq, g_wk, g_wv, d_dealt, g_one = qkv_backward(x_rows, gains[0], d_mid, dq, dk, dv, wq, wk, wv)
+
+    hist = hist[:, :, 0, :]
+    turned = hist[:3, :, ::-1]
+    by_distance = jnp.concatenate([turned[1], jnp.zeros((H, 1), f32)], axis=1)
+    by_distance = by_distance.at[:, 128:256].add(turned[2][:, :128])
+    by_distance = by_distance.at[:, 256].add(jnp.sum(turned[2][:, 128:], axis=1) + jnp.sum(hist[4], axis=1))
+    by_distance = by_distance.at[:, :128].add(turned[0][:, 128:])
+    by_distance = by_distance.at[:, 0].add(jnp.sum(turned[0][:, :128], axis=1) + jnp.sum(hist[3], axis=1))
+    g_rel = lax.dot_general(
+        picked, by_distance, (((1,), (1,)), ((), ())), precision=lax.Precision.HIGHEST, preferred_element_type=f32
+    )
+    wide = lambda v: jnp.pad(v, ((0, 0), (0, 128 - v.shape[1])))[:, None]
+    g_small = jnp.concatenate(
+        [wide(g_one[0].reshape(32, 24)), wide(g_two[0].reshape(32, 24)), wide(g_rel), jnp.zeros((32, 13, 128), f32)],
+        axis=1,
+    ).astype(jnp.bfloat16)
+    split = lambda g: g.reshape(32, -1, g.shape[-1])
+    done = scatter_all(
+        deal_u.reshape(2, 1, -1),
+        result.reshape(OWN, TILE, width),
+        d_dealt.reshape(OWN, TILE, width),
+        (g_small, split(g_wq), split(g_wk), split(g_wv), split(g_wo), split(g_wi), split(g_wu)),
+    )
+    hid, gin, s_small = done[:3]
+    return (
+        hid.astype(f32),
+        gin.reshape(2, tok_rows, width).astype(f32),
+        s_small[0, :24],
+        s_small[1, :24],
+        s_small[2, :H],
+        *done[3:],
+    )
+
+
 def solution(mesh):
-    placed = (
-        P(None, ("dp", "fsdp"), None),
-        P(None, ("dp", "fsdp"), None),
-        P(("dp", "fsdp")),
-        P(("dp", "fsdp")),
-        P(("dp", "fsdp")),
-        P(("dp", "fsdp"), None),
-        P(("dp", "fsdp"), None),
-        P(("dp", "fsdp"), None),
-        P(("dp", "fsdp"), None),
-        P(("dp", "fsdp"), None),
-        P(("dp", "fsdp"), None),
-        P(None, "dp", None),
-        P(None, "dp", None),
-        P(),
-    )
+    axes = ("dp", "fsdp")
+    tokens, matrix, vector = P(None, axes, None), P(axes, None), P(axes)
+    packed = mesh.shape["fsdp"] == 4 and mesh.shape["dp"] == 8
     return jax.shard_map(
-        on_device,
+        on_device_packed if packed else on_device,
         mesh=mesh,
-        in_specs=placed,
-        out_specs=(
-            P(None, ("dp", "fsdp"), None),
-            P(None, ("dp", "fsdp"), None),
-            P(("dp", "fsdp")),
-            P(("dp", "fsdp")),
-            P(("dp", "fsdp")),
-            P(("dp", "fsdp"), None),
-            P(("dp", "fsdp"), None),
-            P(("dp", "fsdp"), None),
-            P(("dp", "fsdp"), None),
-            P(("dp", "fsdp"), None),
-            P(("dp", "fsdp"), None),
-        ),
+        in_specs=(tokens, tokens, vector, vector, vector)
+        + (matrix,) * 6
+        + (P(None, "dp", None), P(None, "dp", None), P()),
+        out_specs=(tokens, tokens, vector, vector, vector) + (matrix,) * 6,
         check_vma=False,
     )

time: 2030 us -> 448 us (0.22)
  waiting for transfers between devices: 875 us -> 0 us
  matrix products: 600 us -> 0.27 us
  Pallas kernels: 0 us -> 410 us
  local copies, waits for them, and re-layouts: 325 us -> 16.2 us
  blocking collectives: 81.9 us -> 0 us
  other arithmetic: 88.1 us -> 10.7 us
    dot_general x102 -> x2, matrix products: 600 us -> 0.27 us  [the longest x1 0.14 us: on_device_packed(): lax.dot_general(picked, by_distance, (((1,), (1,)), ((), ())), precision=...]
    reduce_scatter x6 -> x0, waiting for transfers between devices: 584 us -> none  [the longest x1 142 us: on_device(): lax.psum_scatter(acc_outer, ('dp', 'fsdp'), scatter_dimension=0, tiled=True)]
    pallas_call x0 -> x6, Pallas kernels: none -> 410 us  [the longest x1 138 us: scatter_all(): pl.pallas_call(functools.partial(scatter_kernel, FIRST_AXIS), name='scatt...]
    all_gather x10 -> x0, waiting for transfers between devices: 169 us -> none  [the longest x2 47.4 us: on_device(): lax.all_gather(value_rows, 'fsdp', axis=0, tiled=True)]
    dot_general x12 -> x0, local copies, waits for them, and re-layouts: 143 us -> none  [block_scores(): jnp.einsum('qkb,bh->hqk', bucket_hit, rel_bucket, precision=lax.Precision...]
    unnamed x242 -> x25, local copies, waits for them, and re-layouts: 107 us -> 4 us
    unnamed x24 -> x0, waiting for transfers between devices: 94.4 us -> none
    unnamed x2 -> x0, blocking collectives: 81.9 us -> none
  transfers between devices with their start and end apart: 24 -> 0, of which waited for: 13 -> 0; matrix products, arithmetic and copies ran while one was open for 40% -> 0% of each run, Pallas kernels for 0% -> 0%
where the time goes in v1:
time: 448 us; the launch traced here: 439 us
  Pallas kernels  410 us (92%)
  local copies, waits for them, and re-layouts  16.2 us (4%)
  other arithmetic  10.7 us (2%)
    pallas_call x1, Pallas kernels, scatter_all(): pl.pallas_call(functools.partial(scatter_kernel, FIRST_AXIS), name='scatt...  138 us
    pallas_call x1, Pallas kernels, gather_all(): pl.pallas_call(functools.partial(gather_kernel, FIRST_AXIS), name='gather...  137 us
    pallas_call x1, Pallas kernels, attention_backward(): pl.pallas_call(attn_bwd, name='attn_bwd', out_shape=[shaped(*heads)] * 3...  46.4 us
    pallas_call x1, Pallas kernels, feed_forward(): pl.pallas_call(ffn_kernel, name='feed_forward', grid=(hidden // chunk,),...  40.3 us
    pallas_call x1, Pallas kernels, attention_forward(): pl.pallas_call(attn_fwd, name='attn_fwd', out_shape=[shaped(*heads), shap...  36.7 us
    pallas_call x1, Pallas kernels, qkv_backward(): pl.pallas_call(qkv_back_kernel, name='qkv_back', out_shape=[shaped(width,...  11.9 us

profile of v1, /device:TPU:0, one launch (start us, length us, event | category | flops | bytes accessed | tf_op | source)
XLA Modules:
  0.0 438.9 jit_solution(18091583941347551077)
XLA Ops:
  2.0 1.2 pad.38.refs_0_
  3.3 0.7 pad_bitcast_fusion.3
  4.6 0.7 maximum_maximum_fusion.1.refs_4_
  5.3 137.2 %gather_all.1 = (s32[1,128]{1,0:T(1,128)}, s32[1,1536]{1,0:T(1,128)}, bf16[6,128,768]{2,1,0:T(8,128)(2,1)}, bf16[8,192,768]{2,1,0:T(8,128)(2,1)}, bf16[32,16,128...) custom-call(s32[2,1,128]{2,1,0:T(1,128)} %pad.38.refs_0_, ...), custom_call_target="tpu_custom_call" | custom-call | tf_op jit(solution)/shard_map/gather_all/pallas_call | solution.py:1164
  142.5 0.9 slice.183
  143.4 1.0 convert_reduce_fusion
  146.6 0.7 broadcast_in_dim.46.rows_ref
  147.2 0.7 copy.32.rows_ref
  147.9 36.7 %attn_fwd.1 = (bf16[6,6,128,128]{3,2,1,0:T(8,128)(2,1)}, bf16[6,6,2,128,128]{4,3,2,1,0:T(8,128)(2,1)}, bf16[6,6,2,128,128]{4,3,2,1,0:T(8,128)(2,1)}, f32[6,6,128,128]{3,2,1,0:T(8,128)}, f32[6,12,1,128]{3,2,1,0:T(1,128)}) custom-call(s32[1,128]{1,0:T(1,128)} %get-tuple-element.103.lens_ref, bf16[768,768]{1,0:T(8,128)(2,1)} %bitcast.96, ...), custom_call_target="tpu_custom_call" | custom-call | tf_op jit(solution)/shard_map/attn_fwd/pallas_call | solution.py:1210
  184.6 40.3 %feed_forward.1 = (bf16[768,768]{1,0:T(8,128)(2,1)}, f32[768,768]{1,0:T(8,128)}, bf16[6,6,128,128]{3,2,1,0:T(8,128)(2,1)}, f32[6,12,1,128]{3,2,1,0:T(1,128)}, bf...) custom-call(s32[1,1536]{1,0:T(1,128)} %get-tuple-element.101.deal_ref, ...), custom_call_target="tpu_custom_call" | custom-call | tf_op jit(solution)/shard_map/feed_forward/pallas_call | solution.py:1259
  224.9 46.4 %attn_bwd.1 = (bf16[6,6,128,128]{3,2,1,0:T(8,128)(2,1)}, bf16[6,6,128,128]{3,2,1,0:T(8,128)(2,1)}, bf16[6,6,128,128]{3,2,1,0:T(8,128)(2,1)}, f32[5,12,1,256]{3,2,1,0:T(1,128)}) custom-call(s32[1,128]{1,0:T(1,128)} %get-tuple-element.103.lens_ref, bf16[6,6,128,128]{3,2,1,0:T(8,128)(2,1)} %get-tuple-element.115.q_ref, ...), custom_call_target="tpu_custom_call" | custom-call | tf_op jit(solution)/shard_map/attn_bwd/pallas_call | solution.py:1233
  271.3 11.9 %qkv_back.1 = (bf16[768,768]{1,0:T(8,128)(2,1)}, bf16[768,768]{1,0:T(8,128)(2,1)}, bf16[768,768]{1,0:T(8,128)(2,1)}, bf16[768,768]{1,0:T(8,128)(2,1)}, f32[8,768]{1,0:T(8,128)}) custom-call(bf16[768,768]{1,0:T(8,128)(2,1)} %bitcast.98, f32[8,768]{1,0:T(8,128)} %broadcast_in_dim.39.gain_ref, f32[768,768]{1,0:T(8,128)} %get-tuple-element.114.dmid_ref, ...), custom_call_target="tpu_custom_call" | custom-call | tf_op jit(solution)/shard_map/qkv_back/pallas_call | solution.py:1286
  283.2 0.8 fusion.13
  284.0 0.8 fusion.12
  286.1 0.8 slice_reduce_fusion.3
  286.9 0.8 slice_reduce_fusion.2
  288.8 0.8 maximum_maximum_fusion.refs_3_
  289.6 137.8 %scatter_all.1 = (bf16[2,384,768]{2,1,0:T(8,128)(2,1)}, bf16[2,3,128,768]{3,2,1,0:T(8,128)(2,1)}, f32[16,128]{1,0:T(8,128)}, f32[24,768]{1,0:T(8,128)}, f32[24,7...) custom-call(s32[2,1,768]{2,1,0:T(1,128)} %bitcast.124, ...), custom_call_target="tpu_custom_call" | custom-call | tf_op jit(solution)/shard_map/scatter_all/pallas_call | solution.py:1187
  427.4 1.2 slice_bitcast_fusion.3
  428.6 1.3 slice_bitcast_fusion.4
  429.9 2.9 convert_element_type.48
  432.8 1.7 bitcast_convert_fusion
  437.0 0.7 copy.68
  437.8 0.7 copy.69
  (70 shorter events, 9.1 us)
Async XLA Ops:
  5.2 140.0 %copy-start.8 = (s32[257]{0:T(512)S(1)}, s32[257]{0:T(512)}, u32[]{:S(2)}) copy-start(s32[257]{0:T(512)} %param.35) | copy-start | bytes 3088
  271.3 13.7 %copy-start.3 = (f32[5,12,1,256]{3,2,1,0:T(1,128)S(1)}, f32[5,12,1,256]{3,2,1,0:T(1,128)}, u32[]{:S(2)}) copy-start(f32[5,12,1,256]{3,2,1,0:T(1,128)} %get-tuple-element.127) | copy-start | bytes 184324
  429.9 2.9 copy-start
  432.8 1.7 copy-start.7
  432.8 2.3 copy-start.6
  432.8 3.0 copy-start.5
  432.8 3.6 copy-start.4
  432.8 4.2 copy-start.2
  434.5 3.3 copy-start.1
